TPU v7x, 256 devices: a whole 4x4x8 slice. The times are simulated.
256 devices in a mesh: island: 16 (over y_lo, x, core), fsdp: 16 (over z, y_hi).
Axes of the slice: x: 4, y: 4 (y_hi: 2, y_lo: 2; y = y_hi * 2 + y_lo), z: 8, core: 2. Of those that a mesh axis runs over, the one named last changes fastest.
Arguments:
- tokens: bfloat16 [16, 4096, 8192], P('island', 'fsdp'), may hold values from -6 to 6
- cotangent: bfloat16 [16, 4096, 1024], P('island', 'fsdp'), may hold values from -0.09375 to 0.09375
- params: float32 [16, 8192, 1024], P('island', 'fsdp'), may hold values from -0.18 to 0.18
- first_moment: bfloat16 [16, 8192, 1024], P('island', 'fsdp'), may hold values from -3 to 3
- second_moment: bfloat16 [16, 8192, 1024], P('island', 'fsdp'), may hold values from 0.25 to 4
- base: float32 [8192, 512], P(('fsdp', 'island')), may hold values from -0.18 to 0.18
- outer_momentum: float32 [8192, 512], P(('fsdp', 'island')), may hold values from -0.06 to 0.06
- head_order: int32 [8], replicated, may hold values from 0 to 7, each once
- step_fragment: int32 [1], replicated, may hold values from 0 to 1
Outputs:
- params_out: float32 [16, 8192, 1024], P('island', 'fsdp')
- first_out: bfloat16 [16, 8192, 1024], P('island', 'fsdp')
- second_out: bfloat16 [16, 8192, 1024], P('island', 'fsdp')
- base_out: float32 [8192, 512], P(('fsdp', 'island'))
- momentum_out: float32 [8192, 512], P(('fsdp', 'island'))
All inputs are finite; a program needn't handle non-finite values.
Results may differ from a plain program's by a relative error of at most 0.012.
Values may be sent and summed in bfloat16 or wider, within the bound.
A program may use at most 128 MiB of HBM per device.

v0:
```python
import jax
import jax.numpy as jnp
from jax import lax
from jax.sharding import PartitionSpec as P

KVH = 8
HD = 128
SYNC = 4


def outer_update(base, outer_momentum, total, islands):
    delta = base - total / islands
    momentum = 0.9 * outer_momentum + delta
    return (base - 0.7 * (delta + 0.9 * momentum), momentum)


def shards(
    tokens,
    cotangent,
    params,
    first_moment,
    second_moment,
    base,
    outer_momentum,
    head_order,
    step_fragment,
):
    local_tokens = tokens[0]
    local_grads = cotangent[0]
    weights = params[0]
    rows = weights.shape[0]
    width = weights.shape[1]
    grad = lax.psum_scatter(
        lax.dot_general(
            local_tokens, local_grads, (((0,), (0,)), ((), ())), preferred_element_type=jnp.float32
        ).astype(jnp.bfloat16),
        "fsdp",
        scatter_dimension=0,
        tiled=True,
    ).astype(jnp.float32)
    moment_one = 0.9 * first_moment[0].astype(jnp.float32) + 0.1 * grad
    moment_two = 0.95 * second_moment[0].astype(jnp.float32) + 0.05 * grad * grad
    stepped = weights - 0.01 * (moment_one / (jnp.sqrt(moment_two) + 1e-08) + 0.1 * weights)
    heads = lax.dynamic_slice(head_order, (step_fragment[0] * SYNC,), (SYNC,))
    shaped = stepped.reshape(rows, KVH, HD)
    fragment = jnp.take(shaped, heads, axis=1).reshape(rows, SYNC * HD)
    islands = lax.axis_size("island")
    total = lax.psum_scatter(
        fragment.astype(jnp.bfloat16), "island", scatter_dimension=0, tiled=True
    ).astype(jnp.float32)
    base_next, momentum_next = outer_update(base, outer_momentum, total, islands)
    whole_base = lax.all_gather(
        base_next.astype(jnp.bfloat16), "island", axis=0, tiled=True
    ).astype(base_next.dtype)
    updated = shaped.at[:, heads, :].set(whole_base.reshape(rows, SYNC, HD)).reshape(rows, width)
    return (
        updated[None],
        moment_one.astype(jnp.bfloat16)[None],
        moment_two.astype(jnp.bfloat16)[None],
        base_next,
        momentum_next,
    )


def solution(mesh):
    placed = (
        P("island", "fsdp", None),
        P("island", "fsdp", None),
        P("island", "fsdp", None),
        P("island", "fsdp", None),
        P("island", "fsdp", None),
        P(("fsdp", "island"), None),
        P(("fsdp", "island"), None),
        P(),
        P(),
    )
    return jax.shard_map(
        shards,
        mesh=mesh,
        in_specs=placed,
        out_specs=(
            P("island", "fsdp", None),
            P("island", "fsdp", None),
            P("island", "fsdp", None),
            P(("fsdp", "island"), None),
            P(("fsdp", "island"), None),
        ),
        check_vma=False,
    )
```

profile of v0, /device:TPU:1, one launch (start us, length us, event | category | flops | bytes accessed | tf_op | source)
XLA Modules:
  0.0 413.9 jit_solution(12646848179736934756)
XLA Ops:
  7.2 0.0 copy-start
  7.2 0.0 reduce-scatter.5.cloned.1.call-start
  7.2 1.0 copy-done
  8.2 10.5 %convolution_convert_fusion = bf16[8192,1024]{1,0:T(8,128)(2,1)} fusion(bf16[1,256,8192]{2,1,0:T(8,128)(2,1)} %param.9, bf16[1,256,1024]{2,1,0:T(8,128)(2,1)S(1)} %copy-done), kind=kOutput, calls=%fused_computation.2 | convolution fusion | flops 4303355904 | bytes 21495808 | tf_op jit(solution)/shard_map/dot_general | solution.py:34
  18.7 0.0 copy-start.4
  18.7 0.0 copy-start.1
  18.7 0.0 reduce-scatter.5.cloned.1.call-update
  18.7 0.0 reduce-scatter.7.cloned.1.call-start
  19.5 0.0 copy-done.4
  19.6 0.1 compare_and_fusion
  19.6 0.1 broadcast_bitcast_fusion
  19.7 288.3 %reduce-scatter.5.cloned.1.call-done = bf16[512,1024]{1,0:T(8,128)(2,1)} async-done(((bf16[8192,1024]{1,0:T(8,128)(2,1)}), bf16[512,1024]{1,0:T(8,128)(2,1)}) %reduce-scatter.5.cloned.1.call-update) | async-done | bytes 1048592 | tf_op jit(solution)/shard_map/reduce_scatter | solution.py:33
  308.0 0.0 copy-done.1
  308.0 4.9 %fusion.8 = (bf16[1,512,1024]{2,1,0:T(8,128)(2,1)}, f32[64,8,8,128]{3,2,1,0:T(8,128)S(1)}, bf16[1,512,1024]{2,1,0:T(8,128)(2,1)}) fusion(bf16[512,1024]{1,0:T(8,128)(2,1)} %reduce-scatter.5.cloned.1.call-done, bf16[1,512,1024]{2,1,0:T(8,128)(2,1)} %param.13, bf16[1,512,1024]{2,1,0:T(8,128)(2,1)} %param.12, f32[1,512,1024]{2,1,0:T(8,128)S(1)} %copy-done.1), kind=kLoop, calls=%fused_computation.16 | loop fusion | flops 9437184 | bytes 9437184 | tf_op jit(solution)/shard_map/broadcast_in_dim | solution.py:59
  312.9 0.1 copy.57
  313.0 1.4 gather_fusion
  314.4 0.0 copy-start.2
  314.4 0.0 copy-start.3
  314.4 1.3 copy.45
  315.7 1.0 fusion.10
  316.7 2.0 copy.51
  318.7 0.0 reduce-scatter.7.cloned.1.call-update
  318.7 57.7 %reduce-scatter.7.cloned.1.call-done = bf16[32,512]{1,0:T(8,128)(2,1)} async-done(((bf16[512,512]{1,0:T(8,128)(2,1)}), bf16[32,512]{1,0:T(8,128)(2,1)}) %reduce-scatter.7.cloned.1.call-update) | async-done | bytes 32784 | tf_op jit(solution)/shard_map/reduce_scatter | solution.py:48
  376.4 0.0 copy-done.2
  376.4 0.0 copy-done.3
  376.5 1.4 fusion.12
  377.9 21.4 %all_gather.3 = bf16[512,512]{1,0:T(8,128)(2,1)S(1)} all-gather(bf16[32,512]{1,0:T(8,128)(2,1)S(1)} %get-tuple-element.25), channel_id=1, replica_groups=mesh['island'=16,'fsdp'=16] {'island'}, dimensions={0}, use_global_device_ids=true | all-gather | bytes 557056 | tf_op jit(solution)/shard_map/all_gather | solution.py:52
  399.3 1.0 bitcast_bitcast_fusion
  400.3 1.9 scatter_fusion
  402.3 1.9 copy.49
  404.2 2.9 copy.50
  (1 shorter events, 0.0 us)
Async XLA Ops:
  7.2 1.0 copy-start
  7.2 300.8 %reduce-scatter.5.cloned.1.call-start = ((), (), s32[]{:S(2)}) async-start(), calls=%async_computation.2 | async-start | bytes 17825792 | tf_op jit(solution)/shard_map/reduce_scatter | solution.py:33
  18.7 0.9 copy-start.4
  18.7 289.3 %copy-start.1 = (f32[1,512,1024]{2,1,0:T(8,128)S(1)}, f32[1,512,1024]{2,1,0:T(8,128)}, u32[]{:S(2)}) copy-start(f32[1,512,1024]{2,1,0:T(8,128)} %param.11) | copy-start | bytes 6291460
  18.7 357.7 %reduce-scatter.7.cloned.1.call-start = ((), (), s32[]{:S(2)}) async-start(), calls=%async_computation.3 | async-start | bytes 557056 | tf_op jit(solution)/shard_map/reduce_scatter | solution.py:48
  314.4 62.0 %copy-start.2 = (f32[32,512]{1,0:T(8,128)S(1)}, f32[32,512]{1,0:T(8,128)}, u32[]{:S(2)}) copy-start(f32[32,512]{1,0:T(8,128)} %param.14) | copy-start | bytes 196612
  314.4 62.0 %copy-start.3 = (f32[32,512]{1,0:T(8,128)S(1)}, f32[32,512]{1,0:T(8,128)}, u32[]{:S(2)}) copy-start(f32[32,512]{1,0:T(8,128)} %param.15) | copy-start | bytes 196612
Sparse Core Ops, SparseCore 0:
  18.8 289.1 reduce-scatter.4
  318.9 57.5 reduce-scatter.6
where the time goes:
time: 414 us
  waiting for transfers between devices  346 us (84%)
  blocking collectives  21.4 us (5%)
  between operations  14.9 us (4%)
  local copies, waits for them, and re-layouts  12.6 us (3%)
  matrix products  10.5 us (3%)
  other arithmetic  8.41 us (2%)
    reduce_scatter x1, waiting for transfers between devices, shards(): lax.psum_scatter(lax.dot_general(local_tokens, local_grads, (((0,), (0,))...  288 us
    reduce_scatter x1, waiting for transfers between devices, shards(): lax.psum_scatter(fragment.astype(jnp.bfloat16), 'island', scatter_dimensi...  57.7 us
    all_gather x1, blocking collectives, shards(): lax.all_gather(base_next.astype(jnp.bfloat16), 'island', axis=0, tiled=True)  21.4 us
    dot_general x1, matrix products, shards(): lax.dot_general(local_tokens, local_grads, (((0,), (0,)), ((), ())), pref...  10.5 us
  transfers between devices with their start and end apart: 2, of which 2 were waited for; matrix products, arithmetic and copies ran while one was open for 0% of the time, Pallas kernels for 0%

commit v1 on v0

v1 whole, which is shorter than its diff:
```python
import functools

import jax
import jax.numpy as jnp
from jax import lax
from jax.experimental import pallas as pl
from jax.experimental.pallas import tpu as pltpu
from jax.sharding import PartitionSpec as P

KVH = 8
HD = 128
SYNC = 4
Z = 8
HALF = 256
GC = 256
MESH = pl.DeviceIdType.MESH
F32 = jnp.float32
BF16 = jnp.bfloat16


def partial_product(a, b):
    return lax.dot_general(a, b, (((0,), (0,)), ((), ())), preferred_element_type=F32)


def sync_kernel(
    order_ref,
    step_ref,
    tokens,
    cotangent,
    params,
    first_moment,
    second_moment,
    base,
    outer_momentum,
    out_weights,
    out_first,
    out_second,
    out_base,
    out_momentum,
    cot_raw,
    cot,
    tok,
    tok_stage,
    sent,
    got,
    weights_v,
    first_v,
    second_v,
    base_v,
    outer_v,
    weights_p,
    first_p,
    second_p,
    new_weights,
    new_first,
    new_second,
    frag,
    frag_got,
    base_sent,
    base_all,
    base_new,
    outer_new,
    cot_load,
    own_load,
    stage_load,
    state_load,
    y_send_cot,
    y_recv_cot,
    y_send_tok,
    y_recv_tok,
    z_send,
    z_recv,
    frag_send,
    frag_recv,
    base_send,
    base_recv,
    store_sem,
    weights_store,
    small_store,
):
    island = lax.axis_index("island")
    fsdp = lax.axis_index("fsdp")
    islands = lax.axis_size("island")
    z = fsdp // 2
    h = fsdp % 2
    partner = (island, z * 2 + (1 - h))
    up = (island, ((z + 1) % Z) * 2 + h)
    down = (island, ((z + Z - 1) % Z) * 2 + h)
    deltas = (4, 3, 5, 2, 6, 1, 7, 0)
    token_order = (
        (0, 0), (0, 1), (1, 0), (2, 1), (1, 1), (2, 0), (3, 0), (4, 1),
        (3, 1), (4, 0), (5, 0), (6, 1), (5, 1), (6, 0), (7, 0), (7, 1),
    )

    barrier = pltpu.get_barrier_semaphore()
    for peer in (partner, up, down):
        pl.semaphore_signal(barrier, inc=1, device_id=peer, device_id_type=MESH)

    def greet(k, carry):
        pl.semaphore_signal(
            barrier, inc=1, device_id=(lax.rem(island + k, islands), fsdp), device_id_type=MESH
        )
        return carry

    cot_copy = pltpu.make_async_copy(cotangent, cot_raw, cot_load)
    cot_copy.start()

    def own_copy(s, r):
        column = ((z + deltas[s]) % Z * 2 + h) * 2 * HALF + r * HALF
        return pltpu.make_async_copy(
            tokens.at[:, pl.ds(pl.multiple_of(column, HALF), HALF)],
            tok.at[s, r, pl.ds(0, HALF), :],
            own_load.at[s, r],
        )

    def stage_copy(s, r):
        column = ((z + deltas[s]) % Z * 2 + (1 - h)) * 2 * HALF + r * HALF
        return pltpu.make_async_copy(
            tokens.at[:, pl.ds(pl.multiple_of(column, HALF), HALF)],
            tok_stage.at[s, r],
            stage_load.at[s, r],
        )

    def y_cot(g):
        return pltpu.make_async_remote_copy(
            cot.at[g, pl.ds(0, HALF), :],
            cot.at[g, pl.ds(HALF, HALF), :],
            y_send_cot.at[g],
            y_recv_cot.at[g],
            device_id=partner,
            device_id_type=MESH,
        )

    def y_tok(s, r):
        return pltpu.make_async_remote_copy(
            tok_stage.at[s, r],
            tok.at[s, r, pl.ds(HALF, HALF), :],
            y_send_tok.at[s, r],
            y_recv_tok.at[s, r],
            device_id=partner,
            device_id_type=MESH,
        )

    for s, r in token_order:
        stage_copy(s, r).start()
    for s, r in token_order:
        own_copy(s, r).start()
    state = [
        pltpu.make_async_copy(src, dst, state_load.at[i])
        for i, (src, dst) in enumerate(
            (
                (params, weights_v),
                (first_moment, first_v),
                (second_moment, second_v),
                (base, base_v),
                (outer_momentum, outer_v),
            )
        )
    ]
    for copy in state:
        copy.start()
    lax.fori_loop(1, islands, greet, 0)

    first_part = step_ref[0] == 0

    def head_of(j):
        return jnp.where(first_part, order_ref[j], order_ref[lax.rem(j + SYNC, KVH)])

    def columns_of(head, source, rows):
        found = source[rows, 0:HD]
        for other in range(1, KVH):
            found = lax.select(head == other, source[rows, other * HD : (other + 1) * HD], found)
        return found

    cot_copy.wait()
    for j in range(KVH):
        cot[j // 2, 0:HALF, (j % 2) * HD : (j % 2 + 1) * HD] = columns_of(
            head_of(j), cot_raw, slice(0, HALF)
        )

    pl.semaphore_wait(barrier, 3 + islands - 1)

    def send_tok(pairs):
        for s, r in pairs:
            stage_copy(s, r).wait()
            y_tok(s, r).start()

    y_cot(0).start()
    send_tok(token_order[:2])
    y_cot(1).start()
    send_tok(token_order[2:6])
    y_cot(2).start()
    y_cot(3).start()
    send_tok(token_order[6:])

    def z_copy(way, stage, g, r):
        return pltpu.make_async_remote_copy(
            sent.at[way, stage, g, r],
            got.at[way, stage, g, r],
            z_send.at[way, stage, g, r],
            z_recv.at[way, stage, g, r],
            device_id=(up, down)[way],
            device_id_type=MESH,
        )

    def need_tok(s, r):
        own_copy(s, r).wait()
        y_tok(s, r).wait_recv()

    def need_cot(g):
        y_cot(g).wait_recv()

    def term(s, g, r):
        return partial_product(tok[s, r], cot[g])

    def pass_on(way, stage, s, g, r):
        total = term(s, g, r)
        if stage >= 1:
            z_copy(way, stage - 1, g, r).wait_recv()
            total = total + got[way, stage - 1, g, r].astype(F32)
        sent[way, stage, g, r] = total.astype(BF16)
        z_copy(way, stage, g, r).start()

    def ends(g):
        pass_on(0, 0, 0, g, 0)
        pass_on(1, 0, 0, g, 1)

    def third(first_use, low):
        for i in range(2):
            if first_use:
                need_tok(1, i)
                need_tok(2, 1 - i)

            def body(g, carry, i=i):
                for way, s, r in ((0, 1, i), (1, 2, 1 - i)):
                    if i == 0:
                        pass_on(way, 1, s, g, r)
                    else:
                        sent[way, 1, g, r] = term(s, g, r).astype(BF16)
                        z_copy(way, 1, g, r).start()
                return carry

            lax.fori_loop(low, low + 2, body, 0)

    def middle(stage, first_use, low):
        s_up, s_down = 2 * stage - 1, 2 * stage

        for i in range(2):
            if first_use:
                need_tok(s_up, i)
                need_tok(s_down, 1 - i)

            def body(g, carry, i=i):
                pass_on(0, stage, s_up, g, i)
                pass_on(1, stage, s_down, g, 1 - i)
                return carry

            lax.fori_loop(low, low + 2, body, 0)

    def sort_heads(low):
        def body(item, carry):
            j = low + item // 2
            rows = pl.ds(pl.multiple_of(item % 2 * HALF, HALF), HALF)
            head = head_of(j)
            weights_p[j, rows, :] = columns_of(head, weights_v, rows)
            first_p[j, rows, :] = columns_of(head, first_v, rows)
            second_p[j, rows, :] = columns_of(head, second_v, rows)
            return carry

        lax.fori_loop(0, 2 * SYNC, body, 0)

    def own_rows(low, fragment):
        def body(item, carry):
            r = item // 2
            g = low + item % 2
            rows = pl.ds(pl.multiple_of(r * HALF, HALF), HALF)
            grad = term(7, g, r)
            for way in range(2):
                z_copy(way, 3, g, r).wait_recv()
                grad = grad + got[way, 3, g, r].astype(F32)
            for k in range(2):
                j = 2 * g + k
                part = grad[:, k * HD : (k + 1) * HD]
                one = 0.9 * first_p[j, rows, :].astype(F32) + 0.1 * part
                two = 0.95 * second_p[j, rows, :].astype(F32) + 0.05 * part * part
                weights = weights_p[j, rows, :]
                stepped = weights - 0.01 * (one / (jnp.sqrt(two) + 1e-08) + 0.1 * weights)
                new_first[j, rows, :] = one.astype(BF16)
                new_second[j, rows, :] = two.astype(BF16)
                if fragment:
                    frag[rows, pl.ds(pl.multiple_of(j * HD, HD), HD)] = stepped.astype(BF16)
                else:
                    new_weights[j, rows, :] = stepped
            heads = pl.ds(2 * g, 2)
            pltpu.make_async_copy(
                new_first.at[heads, rows, :], out_first.at[heads, rows, :], store_sem.at[0, g, r]
            ).start()
            pltpu.make_async_copy(
                new_second.at[heads, rows, :], out_second.at[heads, rows, :], store_sem.at[1, g, r]
            ).start()
            if not fragment:
                pltpu.make_async_copy(
                    new_weights.at[heads, rows, :],
                    out_weights.at[heads, rows, :],
                    weights_store.at[g, r],
                ).start()
            return carry

        lax.fori_loop(0, 4, body, 0)

    share = base.shape[0]

    def frag_copy(k):
        peer = lax.rem(island + k, islands)
        return pltpu.make_async_remote_copy(
            frag.at[pl.ds(pl.multiple_of(peer * share, share), share), :],
            frag_got.at[k],
            frag_send.at[k],
            frag_recv.at[k],
            device_id=(peer, fsdp),
            device_id_type=MESH,
        )

    def base_copy(k):
        return pltpu.make_async_remote_copy(
            base_sent,
            base_all.at[pl.ds(pl.multiple_of(island * share, share), share), :],
            base_send.at[k],
            base_recv.at[k],
            device_id=(lax.rem(island + k, islands), fsdp),
            device_id_type=MESH,
        )

    def each_peer(action):
        def body(k, carry):
            action(k)
            return carry

        lax.fori_loop(1, islands, body, 0)

    def outer_step():
        mine = pl.ds(pl.multiple_of(island * share, share), share)

        def add(k, total):
            frag_copy(k).wait_recv()
            return total + frag_got[k].astype(F32)

        total = lax.fori_loop(1, islands, add, frag[mine, :].astype(F32))
        delta = base_v[...] - total / islands
        momentum = 0.9 * outer_v[...] + delta
        following = base_v[...] - 0.7 * (delta + 0.9 * momentum)
        base_sent[...] = following.astype(BF16)
        base_all[mine, :] = following.astype(BF16)
        base_new[...] = following
        outer_new[...] = momentum
        each_peer(lambda k: base_copy(k).start())

    need_cot(0)
    need_tok(0, 0)
    pass_on(0, 0, 0, 0, 0)
    need_tok(0, 1)
    pass_on(1, 0, 0, 0, 1)
    need_cot(1)
    ends(1)
    third(True, 0)
    need_cot(2)
    ends(2)
    need_cot(3)
    ends(3)
    third(False, 2)
    for copy in state:
        copy.wait()
    sort_heads(0)
    middle(2, True, 0)
    middle(3, True, 0)
    middle(2, False, 2)
    sort_heads(SYNC)
    need_tok(7, 0)
    need_tok(7, 1)
    own_rows(0, True)
    each_peer(lambda k: frag_copy(k).start())
    middle(3, False, 2)
    outer_step()
    small = [
        pltpu.make_async_copy(base_new, out_base, small_store.at[0]),
        pltpu.make_async_copy(outer_new, out_momentum, small_store.at[1]),
    ]
    for copy in small:
        copy.start()
    own_rows(2, False)
    each_peer(lambda k: base_copy(k).wait_recv())
    for j in range(SYNC):
        new_weights[j] = base_all[:, j * HD : (j + 1) * HD].astype(F32)
    front = pltpu.make_async_copy(
        new_weights.at[pl.ds(0, SYNC)], out_weights.at[pl.ds(0, SYNC)], small_store.at[2]
    )
    front.start()

    for g in range(4):
        y_cot(g).wait_send()
    for s, r in token_order:
        y_tok(s, r).wait_send()
    for way in range(2):
        for g in range(4):
            z_copy(way, 0, g, way).wait_send()

    def sends(item, carry):
        for way in range(2):
            z_copy(way, 1 + item // 8, item // 2 % 4, item % 2).wait_send()
        return carry

    lax.fori_loop(0, 24, sends, 0)
    each_peer(lambda k: frag_copy(k).wait_send())
    each_peer(lambda k: base_copy(k).wait_send())
    for copy in small:
        copy.wait()

    def stores(item, carry):
        g = item // 2
        r = item % 2
        rows = pl.ds(pl.multiple_of(r * HALF, HALF), HALF)
        heads = pl.ds(2 * g, 2)
        pltpu.make_async_copy(
            new_first.at[heads, rows, :], out_first.at[heads, rows, :], store_sem.at[0, g, r]
        ).wait()
        pltpu.make_async_copy(
            new_second.at[heads, rows, :], out_second.at[heads, rows, :], store_sem.at[1, g, r]
        ).wait()
        return carry

    lax.fori_loop(0, 8, stores, 0)

    def weight_stores(item, carry):
        g = 2 + item // 2
        r = item % 2
        rows = pl.ds(pl.multiple_of(r * HALF, HALF), HALF)
        heads = pl.ds(2 * g, 2)
        pltpu.make_async_copy(
            new_weights.at[heads, rows, :], out_weights.at[heads, rows, :], weights_store.at[g, r]
        ).wait()
        return carry

    lax.fori_loop(0, 4, weight_stores, 0)
    front.wait()


def placing_kernel(
    order_ref, step_ref, weights, first, second, base, momentum, w_out, f_out, s_out, b_out, m_out
):
    for head in range(KVH):
        place = 0
        for j in range(1, KVH):
            found = order_ref[lax.rem(step_ref[0] * SYNC + j, KVH)] == head
            place = place + jnp.where(found, j, 0)
        columns = slice(head * HD, (head + 1) * HD)
        w_out[:, columns] = weights[place]
        f_out[:, columns] = first[place]
        s_out[:, columns] = second[place]

    @pl.when(pl.program_id(0) == 0)
    def _():
        b_out[...] = base[...]
        m_out[...] = momentum[...]


def shards(
    tokens,
    cotangent,
    params,
    first_moment,
    second_moment,
    base,
    outer_momentum,
    head_order,
    step_fragment,
):
    rows, width = params.shape[1:]
    share, columns = base.shape
    islands = lax.axis_size("island")
    smem = pl.BlockSpec(memory_space=pltpu.SMEM)
    anywhere = pl.BlockSpec(memory_space=pl.ANY)
    dma = pltpu.SemaphoreType.DMA
    made = pl.pallas_call(
        sync_kernel,
        name="inner_step_and_outer_sync",
        out_shape=(
            jax.ShapeDtypeStruct((KVH, rows, HD), F32),
            jax.ShapeDtypeStruct((KVH, rows, HD), BF16),
            jax.ShapeDtypeStruct((KVH, rows, HD), BF16),
            jax.ShapeDtypeStruct((share, columns), F32),
            jax.ShapeDtypeStruct((share, columns), F32),
        ),
        in_specs=[smem] * 2 + [anywhere] * 7,
        out_specs=(anywhere,) * 5,
        scratch_shapes=[
            pltpu.VMEM((HALF, width), BF16),
            pltpu.VMEM((4, 2 * HALF, GC), BF16),
            pltpu.VMEM((Z, 2, 2 * HALF, HALF), BF16),
            pltpu.VMEM((Z, 2, HALF, HALF), BF16),
            pltpu.VMEM((2, 4, 4, 2, HALF, GC), BF16),
            pltpu.VMEM((2, 4, 4, 2, HALF, GC), BF16),
            pltpu.VMEM((rows, width), F32),
            pltpu.VMEM((rows, width), BF16),
            pltpu.VMEM((rows, width), BF16),
            pltpu.VMEM((share, columns), F32),
            pltpu.VMEM((share, columns), F32),
            pltpu.VMEM((KVH, rows, HD), F32),
            pltpu.VMEM((KVH, rows, HD), BF16),
            pltpu.VMEM((KVH, rows, HD), BF16),
            pltpu.VMEM((KVH, rows, HD), F32),
            pltpu.VMEM((KVH, rows, HD), BF16),
            pltpu.VMEM((KVH, rows, HD), BF16),
            pltpu.VMEM((rows, columns), BF16),
            pltpu.VMEM((16, share, columns), BF16),
            pltpu.VMEM((share, columns), BF16),
            pltpu.VMEM((rows, columns), BF16),
            pltpu.VMEM((share, columns), F32),
            pltpu.VMEM((share, columns), F32),
            dma,
            dma((Z, 2)),
            dma((Z, 2)),
            dma((5,)),
            dma((4,)),
            dma((4,)),
            dma((Z, 2)),
            dma((Z, 2)),
            dma((2, 4, 4, 2)),
            dma((2, 4, 4, 2)),
            dma((16,)),
            dma((16,)),
            dma((16,)),
            dma((16,)),
            dma((2, 4, 2)),
            dma((4, 2)),
            dma((3,)),
        ],
        compiler_params=pltpu.CompilerParams(
            collective_id=0, has_side_effects=True, vmem_limit_bytes=60 * 2**20
        ),
        cost_estimate=pl.CostEstimate(
            flops=2 * 256 * 8192 * 1024, bytes_accessed=13 * 2**20, transcendentals=rows * width
        ),
    )(
        head_order,
        step_fragment,
        tokens[0],
        cotangent[0],
        params[0],
        first_moment[0],
        second_moment[0],
        base,
        outer_momentum,
    )
    steps = 4
    tall = rows // steps
    block = pl.BlockSpec((KVH, tall, HD), lambda i: (0, i, 0))
    wide = pl.BlockSpec((tall, width), lambda i: (i, 0))
    small = pl.BlockSpec((share, columns), lambda i: (0, 0))
    weights, first, second, base_next, momentum_next = pl.pallas_call(
        placing_kernel,
        name="heads_in_place",
        grid=(steps,),
        out_shape=(
            jax.ShapeDtypeStruct((rows, width), F32),
            jax.ShapeDtypeStruct((rows, width), BF16),
            jax.ShapeDtypeStruct((rows, width), BF16),
            jax.ShapeDtypeStruct((share, columns), F32),
            jax.ShapeDtypeStruct((share, columns), F32),
        ),
        in_specs=[smem, smem, block, block, block, small, small],
        out_specs=(wide, wide, wide, small, small),
        compiler_params=pltpu.CompilerParams(vmem_limit_bytes=16 * 2**20),
    )(head_order, step_fragment, *made)
    return (weights[None], first[None], second[None], base_next, momentum_next)


def solution(mesh):
    placed = (
        P("island", "fsdp", None),
        P("island", "fsdp", None),
        P("island", "fsdp", None),
        P("island", "fsdp", None),
        P("island", "fsdp", None),
        P(("fsdp", "island"), None),
        P(("fsdp", "island"), None),
        P(),
        P(),
    )
    return jax.shard_map(
        shards,
        mesh=mesh,
        in_specs=placed,
        out_specs=(
            P("island", "fsdp", None),
            P("island", "fsdp", None),
            P("island", "fsdp", None),
            P(("fsdp", "island"), None),
            P(("fsdp", "island"), None),
        ),
        check_vma=False,
    )
```

time: 414 us -> 120 us (0.29)
  waiting for transfers between devices: 346 us -> 0 us
  Pallas kernels: 0 us -> 112 us
  blocking collectives: 21.4 us -> 0 us
  between operations: 14.9 us -> 1.32 us
  matrix products: 10.5 us -> 0 us
  other arithmetic: 8.41 us -> 0 us
  local copies, waits for them, and re-layouts: 12.6 us -> 5.71 us
    reduce_scatter x2 -> x0, waiting for transfers between devices: 346 us -> none  [the longest x1 288 us: shards(): lax.psum_scatter(lax.dot_general(local_tokens, local_grads, (((0,), (0,))...]
    pallas_call x0 -> x2, Pallas kernels: none -> 112 us  [the longest x1 109 us: shards(): pl.pallas_call(sync_kernel, name='inner_step_and_outer_sync', out_shape=(...]
    all_gather x1 -> x0, blocking collectives: 21.4 us -> none  [shards(): lax.all_gather(base_next.astype(jnp.bfloat16), 'island', axis=0, tiled=True)]
    dot_general x1 -> x0, matrix products: 10.5 us -> none  [shards(): lax.dot_general(local_tokens, local_grads, (((0,), (0,)), ((), ())), pref...]
    broadcast_in_dim x1 -> x0, other arithmetic: 4.87 us -> none  [shards(): moment_two.astype(jnp.bfloat16)[None]]
  transfers between devices with their start and end apart: 2 -> 0, of which waited for: 2 -> 0; matrix products, arithmetic and copies ran while one was open for 0% -> 0% of each run, Pallas kernels for 0% -> 0%
where the time goes in v1:
time: 120 us
  Pallas kernels  112 us (93%)
  local copies, waits for them, and re-layouts  5.71 us (5%)
  between operations  1.32 us (1%)
    pallas_call x1, Pallas kernels, shards(): pl.pallas_call(sync_kernel, name='inner_step_and_outer_sync', out_shape=(...  109 us
    unnamed x12, local copies, waits for them, and re-layouts  5.71 us
    pallas_call x1, Pallas kernels, shards(): pl.pallas_call(placing_kernel, name='heads_in_place', grid=(steps,), out_...  3.56 us

profile of v1, /device:TPU:1, one launch (start us, length us, event | category | flops | bytes accessed | tf_op | source)
XLA Modules:
  0.0 119.5 jit_solution(12865865592165336186)
XLA Ops:
  1.3 0.0 copy-start.5
  1.3 108.9 %inner_step_and_outer_sync.1 = (f32[8,512,128]{2,1,0:T(8,128)}, bf16[8,512,128]{2,1,0:T(8,128)(2,1)}, bf16[8,512,128]{2,1,0:T(8,128)(2,1)}, f32[32,512]{1,0:T(8,128)}, f32[32,512]{1,0:T(8,128)}) custom-call(s32[8]{0:T(128)} %order_ref.3, s32[1]{0:T(128)S(6)} %copy.14.step_ref, bf16[256,8192]{1,0:T(8,128)(2,1)} %bitcast.8, bf16[256,1024]{1,0:T(8,128)(2,1)} %bitcast.15, ...), custom_call_target="tpu_custom_call" | custom-call | flops 4294967296 | bytes 13631488 | tf_op jit(solution)/shard_map/inner_step_and_outer_sync/pallas_call | solution.py:483
  110.2 0.0 copy-done.5
  110.2 0.0 copy-start
  110.2 1.6 %copy-done = f32[8,512,128]{2,1,0:T(8,128)S(1)} copy-done((f32[8,512,128]{2,1,0:T(8,128)S(1)}, f32[8,512,128]{2,1,0:T(8,128)}, u32[]{:S(2)}) %copy-start) | copy-done | bytes 2097176
  111.8 0.0 copy-start.1
  111.8 1.2 %copy-done.1 = bf16[8,512,128]{2,1,0:T(8,128)(2,1)S(1)} copy-done((bf16[8,512,128]{2,1,0:T(8,128)(2,1)S(1)}, bf16[8,512,128]{2,1,0:T(8,128)(2,1)}, u32[]{:S(2)}) %copy-start.1) | copy-done | bytes 1048600
  113.0 0.0 copy-start.2
  113.0 1.2 %copy-done.2 = bf16[8,512,128]{2,1,0:T(8,128)(2,1)S(1)} copy-done((bf16[8,512,128]{2,1,0:T(8,128)(2,1)S(1)}, bf16[8,512,128]{2,1,0:T(8,128)(2,1)}, u32[]{:S(2)}) %copy-start.2) | copy-done | bytes 1048600
  114.3 0.0 copy-start.3
  114.3 0.8 copy-done.3
  115.1 0.0 copy-start.4
  115.1 0.8 copy-done.4
  115.9 3.6 %heads_in_place.1 = (f32[512,1024]{1,0:T(8,128)}, bf16[512,1024]{1,0:T(8,128)(2,1)}, bf16[512,1024]{1,0:T(8,128)(2,1)}, f32[32,512]{1,0:T(8,128)}, f32[32,512]{1,0:T(8,128)}) custom-call(s32[8]{0:T(128)S(1)} %copy-done.5, s32[1]{0:T(128)S(6)} %copy.14.step_ref, f32[8,512,128]{2,1,0:T(8,128)S(1)} %copy-done, bf16[8,512,128]{2,1,0:T(8,128)(2,1)S(1)} %copy-done.1, ...), custom_call_target="tpu_custom_call" | custom-call | tf_op jit(solution)/shard_map/heads_in_place/pallas_call | solution.py:559
Async XLA Ops:
  1.3 108.9 %copy-start.5 = (s32[8]{0:T(128)S(1)}, s32[8]{0:T(128)}, u32[]{:S(2)}) copy-start(s32[8]{0:T(128)} %order_ref.3) | copy-start | bytes 100
  110.2 1.6 %copy-start = (f32[8,512,128]{2,1,0:T(8,128)S(1)}, f32[8,512,128]{2,1,0:T(8,128)}, u32[]{:S(2)}) copy-start(f32[8,512,128]{2,1,0:T(8,128)} %get-tuple-element.15.weights) | copy-start | bytes 6291460
  111.8 1.2 %copy-start.1 = (bf16[8,512,128]{2,1,0:T(8,128)(2,1)S(1)}, bf16[8,512,128]{2,1,0:T(8,128)(2,1)}, u32[]{:S(2)}) copy-start(bf16[8,512,128]{2,1,0:T(8,128)(2,1)} %get-tuple-element.16.first) | copy-start | bytes 3145732
  113.0 1.2 %copy-start.2 = (bf16[8,512,128]{2,1,0:T(8,128)(2,1)S(1)}, bf16[8,512,128]{2,1,0:T(8,128)(2,1)}, u32[]{:S(2)}) copy-start(bf16[8,512,128]{2,1,0:T(8,128)(2,1)} %get-tuple-element.17.second) | copy-start | bytes 3145732
  114.3 0.8 copy-start.3
  115.1 0.8 copy-start.4

commit v2 on v1

v2 whole, which is shorter than its diff:
```python
import functools

import jax
import jax.numpy as jnp
from jax import lax
from jax.experimental import pallas as pl
from jax.experimental.pallas import tpu as pltpu
from jax.sharding import PartitionSpec as P

KVH = 8
HD = 128
SYNC = 4
Z = 8
HALF = 256
EIGHTH = 128
GC = 256
MESH = pl.DeviceIdType.MESH
F32 = jnp.float32
BF16 = jnp.bfloat16


def partial_product(a, b):
    return lax.dot_general(a, b, (((0,), (0,)), ((), ())), preferred_element_type=F32)


def sync_kernel(
    order,
    step_ref,
    tokens,
    cotangent,
    params,
    first_moment,
    second_moment,
    base,
    outer_momentum,
    new_weights,
    new_first,
    new_second,
    base_new,
    outer_new,
    order_ref,
    cot_raw,
    cot,
    tok,
    tok_stage,
    sent,
    got,
    weights_v,
    first_v,
    second_v,
    base_v,
    outer_v,
    weights_p,
    first_p,
    second_p,
    frag,
    frag_got,
    base_sent,
    base_all,
    plan_load,
    cot_load,
    own_load,
    stage_load,
    state_load,
    y_send_cot,
    y_recv_cot,
    y_send_tok,
    y_recv_tok,
    z_send,
    z_recv,
    frag_send,
    frag_recv,
    base_send,
    base_recv,
):
    island = lax.axis_index("island")
    fsdp = lax.axis_index("fsdp")
    islands = lax.axis_size("island")
    z = fsdp // 2
    h = fsdp % 2
    partner = (island, z * 2 + (1 - h))
    up = (island, ((z + 1) % Z) * 2 + h)
    down = (island, ((z + Z - 1) % Z) * 2 + h)
    deltas = (4, 3, 5, 2, 6, 1, 7, 0)
    token_order = tuple((s, r) for pair in ((0,), (1, 2), (3, 4), (5, 6), (7,)) for r in range(2) for s in pair)

    cot_copy = pltpu.make_async_copy(cotangent, cot_raw, cot_load)

    def own_copy(s, r):
        column = ((z + deltas[s]) % Z * 2 + h) * 2 * HALF + r * HALF
        return pltpu.make_async_copy(
            tokens.at[:, pl.ds(pl.multiple_of(column, HALF), HALF)],
            tok.at[s, r, pl.ds(0, HALF), :],
            own_load.at[s, r],
        )

    def stage_copy(s, r):
        column = ((z + deltas[s]) % Z * 2 + (1 - h)) * 2 * HALF + r * HALF
        return pltpu.make_async_copy(
            tokens.at[:, pl.ds(pl.multiple_of(column, HALF), HALF)],
            tok_stage.at[s, r],
            stage_load.at[s, r],
        )

    def y_cot(g):
        return pltpu.make_async_remote_copy(
            cot.at[g, pl.ds(0, HALF), :],
            cot.at[g, pl.ds(HALF, HALF), :],
            y_send_cot.at[g],
            y_recv_cot.at[g],
            device_id=partner,
            device_id_type=MESH,
        )

    def y_tok(s, r, q=0, size=HALF):
        part = pl.ds(q * EIGHTH, size)
        return pltpu.make_async_remote_copy(
            tok_stage.at[s, r, :, part],
            tok.at[s, r, pl.ds(HALF, HALF), part],
            y_send_tok.at[s, r, q],
            y_recv_tok.at[s, r, q],
            device_id=partner,
            device_id_type=MESH,
        )

    plan = pltpu.make_async_copy(order, order_ref, plan_load)
    plan.start()
    cot_copy.start()
    for s, r in token_order[:2]:
        stage_copy(s, r).start()
    barrier = pltpu.get_barrier_semaphore()
    for peer in (partner, up, down):
        pl.semaphore_signal(barrier, inc=1, device_id=peer, device_id_type=MESH)

    def greet(k, carry):
        pl.semaphore_signal(
            barrier, inc=1, device_id=(lax.rem(island + k, islands), fsdp), device_id_type=MESH
        )
        return carry

    lax.fori_loop(1, islands, greet, 0)
    for s, r in token_order[2:6]:
        stage_copy(s, r).start()
    for s, r in token_order[:2]:
        own_copy(s, r).start()

    plan.wait()
    first_part = step_ref[0] == 0

    def head_of(j):
        return jnp.where(first_part, order_ref[j], order_ref[lax.rem(j + SYNC, KVH)])

    def columns_of(head, source, rows):
        found = source[rows, 0:HD]
        for other in range(1, KVH):
            found = lax.select(head == other, source[rows, other * HD : (other + 1) * HD], found)
        return found

    def sort_cot(g):
        for j in (2 * g, 2 * g + 1):
            cot[g, 0:HALF, (j % 2) * HD : (j % 2 + 1) * HD] = columns_of(
                head_of(j), cot_raw, slice(0, HALF)
            )

    def send_tok(s, r):
        stage_copy(s, r).wait()
        y_tok(s, r).start()

    cot_copy.wait()
    sort_cot(0)
    pl.semaphore_wait(barrier, 3 + islands - 1)
    send_tok(0, 0)
    y_cot(0).start()
    send_tok(0, 1)
    sort_cot(1)
    y_cot(1).start()
    for s, r in token_order[2:6]:
        own_copy(s, r).start()
    for s, r in token_order[6:]:
        stage_copy(s, r).start()
    sort_cot(2)
    sort_cot(3)
    for r in range(2):
        for s in (1, 2):
            stage_copy(s, r).wait()
        for q in range(2):
            for s in (1, 2):
                y_tok(s, r, q, EIGHTH).start()
            if r != q:
                y_cot(2 + r).start()
    for s, r in token_order[6:]:
        own_copy(s, r).start()
    for s, r in token_order[6:]:
        send_tok(s, r)
    state = [
        pltpu.make_async_copy(src, dst, state_load.at[i])
        for i, (src, dst) in enumerate(
            (
                (params, weights_v),
                (first_moment, first_v),
                (second_moment, second_v),
                (base, base_v),
                (outer_momentum, outer_v),
            )
        )
    ]
    for copy in state:
        copy.start()

    def z_copy(way, stage, g, r, low=0, size=HALF):
        rows = pl.ds(low, size)
        return pltpu.make_async_remote_copy(
            sent.at[way, stage, g, r, rows, :],
            got.at[way, stage, g, r, rows, :],
            z_send.at[way, stage, g, r],
            z_recv.at[way, stage, g, r],
            device_id=(up, down)[way],
            device_id_type=MESH,
        )

    def need_tok(s, r):
        own_copy(s, r).wait()
        y_tok(s, r).wait_recv()

    def need_cot(g):
        y_cot(g).wait_recv()

    def term(s, g, r):
        return partial_product(tok[s, r], cot[g])

    def pass_on(way, stage, s, g, r):
        total = term(s, g, r)
        z_copy(way, stage - 1, g, r).wait_recv()
        total = total + got[way, stage - 1, g, r].astype(F32)
        sent[way, stage, g, r] = total.astype(BF16)
        z_copy(way, stage, g, r).start()

    def ends(g, r):
        sent[0, 0, g, r] = term(0, g, r).astype(BF16)
        for way in range(2):
            rows = pl.ds(way * EIGHTH, EIGHTH)
            pltpu.make_async_remote_copy(
                sent.at[0, 0, g, r, rows, :],
                got.at[way, 0, g, r, rows, :],
                z_send.at[way, 0, g, r],
                z_recv.at[way, 0, g, r],
                device_id=(up, down)[way],
                device_id_type=MESH,
            ).start()

    def third_half(way, q, g, r):
        rows = slice(q * EIGHTH, (q + 1) * EIGHTH)
        total = partial_product(tok[1 + way, r, :, rows], cot[g])
        if q == way:
            z_copy(way, 0, g, r, q * EIGHTH, EIGHTH).wait_recv()
            total = total + got[way, 0, g, r, rows, :].astype(F32)
        sent[way, 1, g, r, rows, :] = total.astype(BF16)
        z_copy(way, 1, g, r, q * EIGHTH, EIGHTH).start()

    def third(q, r, low, count):
        def body(g, carry):
            for way in range(2):
                third_half(way, q, g, r)
            return carry

        lax.fori_loop(low, low + count, body, 0)

    def middle_first(stage):
        s_up, s_down = 2 * stage - 1, 2 * stage
        for r in range(2):
            need_tok(s_up, r)
            need_tok(s_down, r)

            def body(g, carry, r=r):
                pass_on(0, stage, s_up, g, r)
                pass_on(1, stage, s_down, g, r)
                return carry

            lax.fori_loop(0, 2, body, 0)

    def middle(stage, g):
        def body(r, carry):
            pass_on(0, stage, 2 * stage - 1, g, r)
            pass_on(1, stage, 2 * stage, g, r)
            return carry

        lax.fori_loop(0, 2, body, 0)

    def sort_heads(low):
        def body(item, carry):
            j = low + item // 2
            rows = pl.ds(pl.multiple_of(item % 2 * HALF, HALF), HALF)
            head = head_of(j)
            weights_p[j, rows, :] = columns_of(head, weights_v, rows)
            first_p[j, rows, :] = columns_of(head, first_v, rows)
            second_p[j, rows, :] = columns_of(head, second_v, rows)
            return carry

        lax.fori_loop(0, 2 * SYNC, body, 0)

    def own_rows(low, fragment, first_item, last_item):
        def body(item, carry):
            r = item % 2
            g = low + item // 2
            rows = pl.ds(pl.multiple_of(r * HALF, HALF), HALF)
            grad = term(7, g, r)
            for way in range(2):
                z_copy(way, 3, g, r).wait_recv()
                grad = grad + got[way, 3, g, r].astype(F32)
            for k in range(2):
                j = 2 * g + k
                part = grad[:, k * HD : (k + 1) * HD]
                one = 0.9 * first_p[j, rows, :].astype(F32) + 0.1 * part
                two = 0.95 * second_p[j, rows, :].astype(F32) + 0.05 * part * part
                weights = weights_p[j, rows, :]
                stepped = weights - 0.01 * (one / (jnp.sqrt(two) + 1e-08) + 0.1 * weights)
                new_first[j, rows, :] = one.astype(BF16)
                new_second[j, rows, :] = two.astype(BF16)
                if fragment:
                    frag[rows, pl.ds(pl.multiple_of(j * HD, HD), HD)] = stepped.astype(BF16)
                else:
                    new_weights[j, rows, :] = stepped
            return carry

        lax.fori_loop(first_item, last_item, body, 0)

    share = base.shape[0]

    def frag_copy(k):
        peer = lax.rem(island + k, islands)
        return pltpu.make_async_remote_copy(
            frag.at[pl.ds(pl.multiple_of(peer * share, share), share), :],
            frag_got.at[k],
            frag_send.at[k],
            frag_recv.at[k],
            device_id=(peer, fsdp),
            device_id_type=MESH,
        )

    def base_copy(k):
        return pltpu.make_async_remote_copy(
            base_sent,
            base_all.at[pl.ds(pl.multiple_of(island * share, share), share), :],
            base_send.at[k],
            base_recv.at[k],
            device_id=(lax.rem(island + k, islands), fsdp),
            device_id_type=MESH,
        )

    def each_peer(action):
        def body(k, carry):
            action(k)
            return carry

        lax.fori_loop(1, islands, body, 0)

    def outer_step():
        mine = pl.ds(pl.multiple_of(island * share, share), share)

        def add(k, total):
            frag_copy(k).wait_recv()
            return total + frag_got[k].astype(F32)

        total = lax.fori_loop(1, islands, add, frag[mine, :].astype(F32))
        delta = base_v[...] - total / islands
        momentum = 0.9 * outer_v[...] + delta
        following = base_v[...] - 0.7 * (delta + 0.9 * momentum)
        base_sent[...] = following.astype(BF16)
        base_all[mine, :] = following.astype(BF16)
        base_new[...] = following
        outer_new[...] = momentum
        each_peer(lambda k: base_copy(k).start())

    need_cot(0)
    for r in range(2):
        need_tok(0, r)
        ends(0, r)
    need_cot(1)
    for r in range(2):
        ends(1, r)

    def need_third(q, r):
        for s in (1, 2):
            if q == 0:
                own_copy(s, r).wait()
            y_tok(s, r, q, EIGHTH).wait_recv()

    for q in range(2):
        need_third(q, 0)
        third(q, 0, 0, 2)
    need_cot(2)
    for r in range(2):
        ends(2, r)
    for q in range(2):
        third(q, 0, 2, 1)
    for q in range(2):
        need_third(q, 1)
        third(q, 1, 0, 3)
    need_cot(3)
    for r in range(2):
        ends(3, r)
    for copy in state:
        copy.wait()
    sort_heads(0)
    middle_first(2)
    middle_first(3)
    for r in range(2):
        for q in range(2):
            third(q, r, 3, 1)
    middle(2, 2)
    sort_heads(SYNC)
    need_tok(7, 0)
    need_tok(7, 1)
    own_rows(0, True, 0, 4)
    each_peer(lambda k: frag_copy(k).start())
    middle(2, 3)
    middle(3, 2)
    outer_step()
    middle(3, 3)
    own_rows(2, False, 0, 2)
    each_peer(lambda k: base_copy(k).wait_recv())
    for j in range(SYNC):
        new_weights[j] = base_all[:, j * HD : (j + 1) * HD].astype(F32)
    own_rows(2, False, 2, 4)

    for g in range(4):
        y_cot(g).wait_send()
    for s, r in token_order:
        if s in (1, 2):
            for q in range(2):
                y_tok(s, r, q, EIGHTH).wait_send()
        else:
            y_tok(s, r).wait_send()

    def leaf_sends(item, carry):
        for way in range(2):
            z_copy(way, 0, item // 2, item % 2, way * EIGHTH, EIGHTH).wait_send()
        return carry

    lax.fori_loop(0, 8, leaf_sends, 0)

    def sends(item, carry):
        for way in range(2):
            z_copy(way, 1 + item // 8, item // 2 % 4, item % 2).wait_send()
        return carry

    lax.fori_loop(0, 24, sends, 0)
    each_peer(lambda k: frag_copy(k).wait_send())
    each_peer(lambda k: base_copy(k).wait_send())


def placing_kernel(
    order,
    step_ref,
    weights,
    first,
    second,
    base,
    momentum,
    w_out,
    f_out,
    s_out,
    b_out,
    m_out,
    order_ref,
    plan_load,
    sems,
):
    plan = pltpu.make_async_copy(order, order_ref, plan_load)
    plan.start()
    copies = []
    for i, (source, out) in enumerate(((base, b_out), (momentum, m_out))):
        copies.append(pltpu.make_async_copy(source, out, sems.at[3, i]))
        copies[-1].start()
    plan.wait()
    for head in range(KVH):
        place = 0
        for j in range(1, KVH):
            found = order_ref[lax.rem(step_ref[0] * SYNC + j, KVH)] == head
            place = place + jnp.where(found, j, 0)
        columns = pl.ds(head * HD, HD)
        for i, (source, out) in enumerate(((weights, w_out), (first, f_out), (second, s_out))):
            copies.append(
                pltpu.make_async_copy(source.at[place], out.at[:, columns], sems.at[i, head])
            )
            copies[-1].start()
    for copy in copies:
        copy.wait()


def shards(
    tokens,
    cotangent,
    params,
    first_moment,
    second_moment,
    base,
    outer_momentum,
    head_order,
    step_fragment,
):
    rows, width = params.shape[1:]
    share, columns = base.shape
    islands = lax.axis_size("island")
    smem = pl.BlockSpec(memory_space=pltpu.SMEM)
    anywhere = pl.BlockSpec(memory_space=pl.ANY)
    dma = pltpu.SemaphoreType.DMA

    def in_hbm(x):
        return pltpu.with_memory_space_constraint(x, pltpu.HBM)

    made = pl.pallas_call(
        sync_kernel,
        name="inner_step_and_outer_sync",
        out_shape=(
            pltpu.VMEM((KVH, rows, HD), F32),
            pltpu.VMEM((KVH, rows, HD), BF16),
            pltpu.VMEM((KVH, rows, HD), BF16),
            pltpu.VMEM((share, columns), F32),
            pltpu.VMEM((share, columns), F32),
        ),
        in_specs=[anywhere, smem] + [anywhere] * 7,
        out_specs=(pl.BlockSpec(memory_space=pltpu.VMEM),) * 5,
        scratch_shapes=[
            pltpu.SMEM((KVH,), jnp.int32),
            pltpu.VMEM((HALF, width), BF16),
            pltpu.VMEM((4, 2 * HALF, GC), BF16),
            pltpu.VMEM((Z, 2, 2 * HALF, HALF), BF16),
            pltpu.VMEM((Z, 2, HALF, HALF), BF16),
            pltpu.VMEM((2, 4, 4, 2, HALF, GC), BF16),
            pltpu.VMEM((2, 4, 4, 2, HALF, GC), BF16),
            pltpu.VMEM((rows, width), F32),
            pltpu.VMEM((rows, width), BF16),
            pltpu.VMEM((rows, width), BF16),
            pltpu.VMEM((share, columns), F32),
            pltpu.VMEM((share, columns), F32),
            pltpu.VMEM((KVH, rows, HD), F32),
            pltpu.VMEM((KVH, rows, HD), BF16),
            pltpu.VMEM((KVH, rows, HD), BF16),
            pltpu.VMEM((rows, columns), BF16),
            pltpu.VMEM((16, share, columns), BF16),
            pltpu.VMEM((share, columns), BF16),
            pltpu.VMEM((rows, columns), BF16),
            dma,
            dma,
            dma((Z, 2)),
            dma((Z, 2)),
            dma((5,)),
            dma((4,)),
            dma((4,)),
            dma((Z, 2, 2)),
            dma((Z, 2, 2)),
            dma((2, 4, 4, 2)),
            dma((2, 4, 4, 2)),
            dma((16,)),
            dma((16,)),
            dma((16,)),
            dma((16,)),
        ],
        compiler_params=pltpu.CompilerParams(
            collective_id=0, has_side_effects=True, vmem_limit_bytes=48 * 2**20
        ),
        cost_estimate=pl.CostEstimate(
            flops=2 * 256 * 8192 * 1024, bytes_accessed=13 * 2**20, transcendentals=rows * width
        ),
    )(
        in_hbm(head_order),
        step_fragment,
        in_hbm(tokens[0]),
        in_hbm(cotangent[0]),
        in_hbm(params[0]),
        in_hbm(first_moment[0]),
        in_hbm(second_moment[0]),
        in_hbm(base),
        in_hbm(outer_momentum),
    )
    weights, first, second, base_next, momentum_next = pl.pallas_call(
        placing_kernel,
        name="heads_in_place",
        out_shape=(
            jax.ShapeDtypeStruct((rows, width), F32),
            jax.ShapeDtypeStruct((rows, width), BF16),
            jax.ShapeDtypeStruct((rows, width), BF16),
            jax.ShapeDtypeStruct((share, columns), F32),
            jax.ShapeDtypeStruct((share, columns), F32),
        ),
        in_specs=[anywhere, smem] + [anywhere] * 5,
        out_specs=(anywhere,) * 5,
        scratch_shapes=[
            pltpu.SMEM((KVH,), jnp.int32),
            dma,
            dma((4, KVH)),
        ],
        compiler_params=pltpu.CompilerParams(vmem_limit_bytes=4 * 2**20),
    )(
        in_hbm(head_order),
        step_fragment,
        *(pltpu.with_memory_space_constraint(x, pltpu.VMEM) for x in made),
    )
    return (weights[None], first[None], second[None], base_next, momentum_next)


def solution(mesh):
    placed = (
        P("island", "fsdp", None),
        P("island", "fsdp", None),
        P("island", "fsdp", None),
        P("island", "fsdp", None),
        P("island", "fsdp", None),
        P(("fsdp", "island"), None),
        P(("fsdp", "island"), None),
        P(),
        P(),
    )
    return jax.shard_map(
        shards,
        mesh=mesh,
        in_specs=placed,
        out_specs=(
            P("island", "fsdp", None),
            P("island", "fsdp", None),
            P("island", "fsdp", None),
            P(("fsdp", "island"), None),
            P(("fsdp", "island"), None),
        ),
        check_vma=False,
    )
```

time: 120 us -> 110 us (0.917)
  local copies, waits for them, and re-layouts: 5.71 us -> 0 us
  Pallas kernels: 112 us -> 109 us
    unnamed x12 -> x0, local copies, waits for them, and re-layouts: 5.71 us -> none
    pallas_call x1, Pallas kernels: 109 us -> 106 us  [shards(): pl.pallas_call(sync_kernel, name='inner_step_and_outer_sync', out_shape=(...]
where the time goes in v2:
time: 110 us
  Pallas kernels  109 us (99%)
  between operations  1.29 us (1%)
    pallas_call x1, Pallas kernels, shards(): pl.pallas_call(sync_kernel, name='inner_step_and_outer_sync', out_shape=(...  106 us
    pallas_call x1, Pallas kernels, shards(): pl.pallas_call(placing_kernel, name='heads_in_place', out_shape=(jax.Shap...  2.97 us

profile of v2, /device:TPU:1, one launch (start us, length us, event | category | flops | bytes accessed | tf_op | source)
XLA Modules:
  0.0 109.9 jit_solution(10885336082423393108)
XLA Ops:
  1.3 105.7 %inner_step_and_outer_sync.1 = (f32[8,512,128]{2,1,0:T(8,128)S(1)}, bf16[8,512,128]{2,1,0:T(8,128)(2,1)S(1)}, bf16[8,512,128]{2,1,0:T(8,128)(2,1)S(1)}, f32[32,512]{1,0:T(8,128)S(1)}, f32[32,512]{1,0:T(8,128)S(1)}) custom-call(s32[8]{0:T(128)} %order.3, s32[1]{0:T(128)S(6)} %copy.14.step_ref, bf16[256,8192]{1,0:T(8,128)(2,1)} %bitcast.8, ...), custom_call_target="tpu_custom_call" | custom-call | flops 4294967296 | bytes 13631488 | tf_op jit(solution)/shard_map/inner_step_and_outer_sync/pallas_call | solution.py:512
  106.9 3.0 %heads_in_place.1 = (f32[512,1024]{1,0:T(8,128)}, bf16[512,1024]{1,0:T(8,128)(2,1)}, bf16[512,1024]{1,0:T(8,128)(2,1)}, f32[32,512]{1,0:T(8,128)}, f32[32,512]{1,0:T(8,128)}) custom-call(s32[8]{0:T(128)} %order.3, s32[1]{0:T(128)S(6)} %copy.14.step_ref, f32[8,512,128]{2,1,0:T(8,128)S(1)} %get-tuple-element.15.weights, ...), custom_call_target="tpu_custom_call" | custom-call | tf_op jit(solution)/shard_map/heads_in_place/pallas_call | solution.py:577

commit v3 on v2

--- a/solution.py
+++ b/solution.py
@@ -45,6 +45,9 @@
     tok_stage,
     sent,
     got,
+    side_sent,
+    side_got,
+    side_all,
     weights_v,
     first_v,
     second_v,
@@ -68,6 +71,10 @@
     y_recv_tok,
     z_send,
     z_recv,
+    side_send,
+    side_recv,
+    cross_send,
+    cross_recv,
     frag_send,
     frag_recv,
     base_send,
@@ -156,6 +163,48 @@
             found = lax.select(head == other, source[rows, other * HD : (other + 1) * HD], found)
         return found
 
+    def side_copy(way, r):
+        return pltpu.make_async_remote_copy(
+            side_sent.at[r, pl.ds(way * EIGHTH, EIGHTH), :],
+            side_got.at[way, r],
+            side_send.at[way, r],
+            side_recv.at[way, r],
+            device_id=(up, down)[way],
+            device_id_type=MESH,
+        )
+
+    def cross_copy(way, r):
+        return pltpu.make_async_remote_copy(
+            side_got.at[way, r],
+            side_all.at[way, r],
+            cross_send.at[way, r],
+            cross_recv.at[way, r],
+            device_id=partner,
+            device_id_type=MESH,
+        )
+
+    def leaf_copy(way, g, r):
+        rows = pl.ds(way * EIGHTH, EIGHTH)
+        return pltpu.make_async_remote_copy(
+            sent.at[0, 0, g, r, rows, :],
+            got.at[way, 0, g, r, rows, :],
+            z_send.at[way, 0, g, r],
+            z_recv.at[way, 0, g, r],
+            device_id=(up, down)[way],
+            device_id_type=MESH,
+        )
+
+    def early_ends(g):
+        for r in range(2):
+            own_copy(0, r).wait()
+            mine = cot[g, 0:HALF, :]
+            sent[0, 0, g, r] = partial_product(tok[0, r, 0:HALF, :], mine).astype(BF16)
+            for way in range(2):
+                leaf_copy(way, g, r).start()
+            side_sent[r] = partial_product(tok_stage[0, r], mine).astype(BF16)
+            for way in range(2):
+                side_copy(way, r).start()
+
     def sort_cot(g):
         for j in (2 * g, 2 * g + 1):
             cot[g, 0:HALF, (j % 2) * HD : (j % 2 + 1) * HD] = columns_of(
@@ -174,12 +223,13 @@
     send_tok(0, 1)
     sort_cot(1)
     y_cot(1).start()
+    sort_cot(3)
+    early_ends(3)
     for s, r in token_order[2:6]:
         own_copy(s, r).start()
     for s, r in token_order[6:]:
         stage_copy(s, r).start()
     sort_cot(2)
-    sort_cot(3)
     for r in range(2):
         for s in (1, 2):
             stage_copy(s, r).wait()
@@ -190,7 +240,7 @@
                 y_cot(2 + r).start()
     for s, r in token_order[6:]:
         own_copy(s, r).start()
-    for s, r in token_order[6:]:
+    for s, r in token_order[6:14]:
         send_tok(s, r)
     state = [
         pltpu.make_async_copy(src, dst, state_load.at[i])
@@ -238,29 +288,24 @@
     def ends(g, r):
         sent[0, 0, g, r] = term(0, g, r).astype(BF16)
         for way in range(2):
-            rows = pl.ds(way * EIGHTH, EIGHTH)
-            pltpu.make_async_remote_copy(
-                sent.at[0, 0, g, r, rows, :],
-                got.at[way, 0, g, r, rows, :],
-                z_send.at[way, 0, g, r],
-                z_recv.at[way, 0, g, r],
-                device_id=(up, down)[way],
-                device_id_type=MESH,
-            ).start()
-
-    def third_half(way, q, g, r):
+            leaf_copy(way, g, r).start()
+
+    def third_half(way, q, g, r, early):
         rows = slice(q * EIGHTH, (q + 1) * EIGHTH)
         total = partial_product(tok[1 + way, r, :, rows], cot[g])
         if q == way:
             z_copy(way, 0, g, r, q * EIGHTH, EIGHTH).wait_recv()
             total = total + got[way, 0, g, r, rows, :].astype(F32)
+            if early:
+                cross_copy(way, r).wait_recv()
+                total = total + side_all[way, r].astype(F32)
         sent[way, 1, g, r, rows, :] = total.astype(BF16)
         z_copy(way, 1, g, r, q * EIGHTH, EIGHTH).start()
 
-    def third(q, r, low, count):
+    def third(q, r, low, count, early=False):
         def body(g, carry):
             for way in range(2):
-                third_half(way, q, g, r)
+                third_half(way, q, g, r, early)
             return carry
 
         lax.fori_loop(low, low + count, body, 0)
@@ -373,7 +418,7 @@
 
     need_cot(0)
     for r in range(2):
-        need_tok(0, r)
+        y_tok(0, r).wait_recv()
         ends(0, r)
     need_cot(1)
     for r in range(2):
@@ -388,6 +433,12 @@
     for q in range(2):
         need_third(q, 0)
         third(q, 0, 0, 2)
+    for r in range(2):
+        for way in range(2):
+            side_copy(way, r).wait_recv()
+            cross_copy(way, r).start()
+    for r in range(2):
+        send_tok(7, r)
     need_cot(2)
     for r in range(2):
         ends(2, r)
@@ -397,8 +448,6 @@
         need_third(q, 1)
         third(q, 1, 0, 3)
     need_cot(3)
-    for r in range(2):
-        ends(3, r)
     for copy in state:
         copy.wait()
     sort_heads(0)
@@ -406,7 +455,7 @@
     middle_first(3)
     for r in range(2):
         for q in range(2):
-            third(q, r, 3, 1)
+            third(q, r, 3, 1, True)
     middle(2, 2)
     sort_heads(SYNC)
     need_tok(7, 0)
@@ -431,6 +480,11 @@
                 y_tok(s, r, q, EIGHTH).wait_send()
         else:
             y_tok(s, r).wait_send()
+
+    for r in range(2):
+        for way in range(2):
+            side_copy(way, r).wait_send()
+            cross_copy(way, r).wait_send()
 
     def leaf_sends(item, carry):
         for way in range(2):
@@ -529,6 +583,9 @@
             pltpu.VMEM((Z, 2, HALF, HALF), BF16),
             pltpu.VMEM((2, 4, 4, 2, HALF, GC), BF16),
             pltpu.VMEM((2, 4, 4, 2, HALF, GC), BF16),
+            pltpu.VMEM((2, HALF, GC), BF16),
+            pltpu.VMEM((2, 2, EIGHTH, GC), BF16),
+            pltpu.VMEM((2, 2, EIGHTH, GC), BF16),
             pltpu.VMEM((rows, width), F32),
             pltpu.VMEM((rows, width), BF16),
             pltpu.VMEM((rows, width), BF16),
@@ -552,6 +609,10 @@
             dma((Z, 2, 2)),
             dma((2, 4, 4, 2)),
             dma((2, 4, 4, 2)),
+            dma((2, 2)),
+            dma((2, 2)),
+            dma((2, 2)),
+            dma((2, 2)),
             dma((16,)),
             dma((16,)),
             dma((16,)),

time: 110 us -> 108 us (0.982)
  Pallas kernels: 109 us -> 106 us
    pallas_call x1, Pallas kernels: 106 us -> 103 us  [shards(): pl.pallas_call(sync_kernel, name='inner_step_and_outer_sync', out_shape=(...]
where the time goes in v3:
time: 108 us; the launch traced here: 107 us
  Pallas kernels  106 us (98%)
  between operations  1.29 us (1%)
    pallas_call x1, Pallas kernels, shards(): pl.pallas_call(sync_kernel, name='inner_step_and_outer_sync', out_shape=(...  103 us
    pallas_call x1, Pallas kernels, shards(): pl.pallas_call(placing_kernel, name='heads_in_place', out_shape=(jax.Shap...  2.97 us

profile of v3, /device:TPU:1, one launch (start us, length us, event | category | flops | bytes accessed | tf_op | source)
XLA Modules:
  0.0 107.5 jit_solution(806570832690976925)
XLA Ops:
  1.3 103.2 %inner_step_and_outer_sync.1 = (f32[8,512,128]{2,1,0:T(8,128)S(1)}, bf16[8,512,128]{2,1,0:T(8,128)(2,1)S(1)}, bf16[8,512,128]{2,1,0:T(8,128)(2,1)S(1)}, f32[32,512]{1,0:T(8,128)S(1)}, f32[32,512]{1,0:T(8,128)S(1)}) custom-call(s32[8]{0:T(128)} %order.3, s32[1]{0:T(128)S(6)} %copy.14.step_ref, bf16[256,8192]{1,0:T(8,128)(2,1)} %bitcast.8, ...), custom_call_target="tpu_custom_call" | custom-call | flops 4294967296 | bytes 13631488 | tf_op jit(solution)/shard_map/inner_step_and_outer_sync/pallas_call | solution.py:566
  104.5 3.0 %heads_in_place.1 = (f32[512,1024]{1,0:T(8,128)}, bf16[512,1024]{1,0:T(8,128)(2,1)}, bf16[512,1024]{1,0:T(8,128)(2,1)}, f32[32,512]{1,0:T(8,128)}, f32[32,512]{1,0:T(8,128)}) custom-call(s32[8]{0:T(128)} %order.3, s32[1]{0:T(128)S(6)} %copy.14.step_ref, f32[8,512,128]{2,1,0:T(8,128)S(1)} %get-tuple-element.15.weights, ...), custom_call_target="tpu_custom_call" | custom-call | tf_op jit(solution)/shard_map/heads_in_place/pallas_call | solution.py:638

commit v4 on v3

--- a/solution.py
+++ b/solution.py
@@ -300,7 +300,8 @@
                 cross_copy(way, r).wait_recv()
                 total = total + side_all[way, r].astype(F32)
         sent[way, 1, g, r, rows, :] = total.astype(BF16)
-        z_copy(way, 1, g, r, q * EIGHTH, EIGHTH).start()
+        if not early:
+            z_copy(way, 1, g, r, q * EIGHTH, EIGHTH).start()
 
     def third(q, r, low, count, early=False):
         def body(g, carry):
@@ -323,10 +324,40 @@
 
             lax.fori_loop(0, 2, body, 0)
 
-    def middle(stage, g):
+    def joined(way, stage, g):
+        return pltpu.make_async_remote_copy(
+            sent.at[way, stage, g],
+            got.at[way, stage, g],
+            z_send.at[way, stage, g, 0],
+            z_recv.at[way, stage, g, 0],
+            device_id=(up, down)[way],
+            device_id_type=MESH,
+        )
+
+    def second(g, came_joined):
+        for way in range(2):
+            if came_joined:
+                joined(way, 1, g).wait_recv()
+
+            def body(r, carry, way=way):
+                total = term(3 + way, g, r)
+                if not came_joined:
+                    z_copy(way, 1, g, r).wait_recv()
+                sent[way, 2, g, r] = (total + got[way, 1, g, r].astype(F32)).astype(BF16)
+                return carry
+
+            lax.fori_loop(0, 2, body, 0)
+            joined(way, 2, g).start()
+
+    def last(g):
+        for way in range(2):
+            joined(way, 2, g).wait_recv()
+
         def body(r, carry):
-            pass_on(0, stage, 2 * stage - 1, g, r)
-            pass_on(1, stage, 2 * stage, g, r)
+            for way in range(2):
+                total = term(5 + way, g, r) + got[way, 2, g, r].astype(F32)
+                sent[way, 3, g, r] = total.astype(BF16)
+                z_copy(way, 3, g, r).start()
             return carry
 
         lax.fori_loop(0, 2, body, 0)
@@ -456,16 +487,18 @@
     for r in range(2):
         for q in range(2):
             third(q, r, 3, 1, True)
-    middle(2, 2)
+    for way in range(2):
+        joined(way, 1, 3).start()
+    second(2, False)
     sort_heads(SYNC)
     need_tok(7, 0)
     need_tok(7, 1)
     own_rows(0, True, 0, 4)
     each_peer(lambda k: frag_copy(k).start())
-    middle(2, 3)
-    middle(3, 2)
+    second(3, True)
+    last(2)
     outer_step()
-    middle(3, 3)
+    last(3)
     own_rows(2, False, 0, 2)
     each_peer(lambda k: base_copy(k).wait_recv())
     for j in range(SYNC):
@@ -494,11 +527,17 @@
     lax.fori_loop(0, 8, leaf_sends, 0)
 
     def sends(item, carry):
+        r = item % 2
         for way in range(2):
-            z_copy(way, 1 + item // 8, item // 2 % 4, item % 2).wait_send()
+            for stage, groups in ((1, (0, 1, 2)), (2, (0, 1)), (3, (0, 1, 2, 3))):
+                for g in groups:
+                    z_copy(way, stage, g, r).wait_send()
         return carry
 
-    lax.fori_loop(0, 24, sends, 0)
+    lax.fori_loop(0, 2, sends, 0)
+    for way in range(2):
+        for stage, g in ((1, 3), (2, 2), (2, 3)):
+            joined(way, stage, g).wait_send()
     each_peer(lambda k: frag_copy(k).wait_send())
     each_peer(lambda k: base_copy(k).wait_send())
 

time: 108 us -> 108 us (level)
  no operation moved by 1% of the time
where the time goes in v4:
time: 108 us; the launch traced here: 107 us
  Pallas kernels  106 us (98%)
  between operations  1.29 us (1%)
    pallas_call x1, Pallas kernels, shards(): pl.pallas_call(sync_kernel, name='inner_step_and_outer_sync', out_shape=(...  103 us
    pallas_call x1, Pallas kernels, shards(): pl.pallas_call(placing_kernel, name='heads_in_place', out_shape=(jax.Shap...  2.97 us

profile of v4, /device:TPU:1, one launch (start us, length us, event | category | flops | bytes accessed | tf_op | source)
XLA Modules:
  0.0 107.4 jit_solution(5341806666599994849)
XLA Ops:
  1.3 103.1 %inner_step_and_outer_sync.1 = (f32[8,512,128]{2,1,0:T(8,128)S(1)}, bf16[8,512,128]{2,1,0:T(8,128)(2,1)S(1)}, bf16[8,512,128]{2,1,0:T(8,128)(2,1)S(1)}, f32[32,512]{1,0:T(8,128)S(1)}, f32[32,512]{1,0:T(8,128)S(1)}) custom-call(s32[8]{0:T(128)} %order.3, s32[1]{0:T(128)S(6)} %copy.14.step_ref, bf16[256,8192]{1,0:T(8,128)(2,1)} %bitcast.8, ...), custom_call_target="tpu_custom_call" | custom-call | flops 4294967296 | bytes 13631488 | tf_op jit(solution)/shard_map/inner_step_and_outer_sync/pallas_call | solution.py:605
  104.4 3.0 %heads_in_place.1 = (f32[512,1024]{1,0:T(8,128)}, bf16[512,1024]{1,0:T(8,128)(2,1)}, bf16[512,1024]{1,0:T(8,128)(2,1)}, f32[32,512]{1,0:T(8,128)}, f32[32,512]{1,0:T(8,128)}) custom-call(s32[8]{0:T(128)} %order.3, s32[1]{0:T(128)S(6)} %copy.14.step_ref, f32[8,512,128]{2,1,0:T(8,128)S(1)} %get-tuple-element.15.weights, ...), custom_call_target="tpu_custom_call" | custom-call | tf_op jit(solution)/shard_map/heads_in_place/pallas_call | solution.py:677
